TPU v7x, 256 devices: a whole 4x4x8 slice. The times are simulated.
256 devices in a mesh: dp: 64 (over z_lo, y, x), mp: 4 (over z_hi, core).
Axes of the slice: x: 4, y: 4, z: 8 (z_hi: 2, z_lo: 4; z = z_hi * 4 + z_lo), core: 2. Of those that a mesh axis runs over, the one named last changes fastest.
Arguments:
- tokens: bfloat16 [16384, 8192], P('dp', 'mp'), may hold values from -8 to 8
- attn_gain: bfloat16 [8192], replicated, may hold values from 0.5 to 1.5
- w_query: bfloat16 [8192, 4096], P('dp', 'mp'), may hold values from -2 to 2
- key_projection_weight: bfloat16 [8192, 512], P('dp', 'mp'), may hold values from -2 to 2
- value_projection_weight: bfloat16 [8192, 512], P('dp', 'mp'), may hold values from -0.0625 to 0.0625
- w_out: bfloat16 [4096, 8192], P('mp', 'dp'), may hold values from -0.09375 to 0.09375
- final_gain: bfloat16 [8192], P('mp'), may hold values from 0.5 to 1.5
- unembed: bfloat16 [64128, 8192], P('dp', 'mp'), may hold values from -0.29882812 to 0.29882812
- clean_ids: int32 [64], replicated, may hold values from 0 to 64127, as said below
- corrupt_ids: int32 [64], replicated, may hold values from 0 to 64127
Outputs:
- head_out: bfloat16 [16384, 4096], P('dp', 'mp')
- scores: float32 [64, 32], P('dp', 'mp')
- metric: float32 [64], P('dp')
Inputs may be any that keep to these rules, and one draw needn't show every extreme that they name: `clean_ids`: split the ids into 64 aligned blocks of equal size and number the groups of 1 sequence alike; the block of a clean answer, minus the number of its sequence's group, taken modulo the number of blocks, is drawn so that every such offset occurs for some sequence.
All inputs are finite; a program needn't handle non-finite values.
Results may differ from a plain program's by a relative error of at most 0.015.
Values may be sent and summed in bfloat16 or wider, within the bound.
No kernel may reach another device: no remote copies, remote signals or barrier semaphores. Data moves between devices by JAX's collectives and lax.ppermute only.
A program may use at most 128 MiB of HBM per device.

v0:
```python
import math
import jax
import jax.numpy as jnp
from jax import lax
from jax.sharding import PartitionSpec as P

MODEL_WIDTH = 8192
HEAD_SIZE = 128
SEQUENCE_LENGTH = 256


def side_by_side(arrays, axis, dim, along):
    ends, at = ([], 0)
    for a in arrays[:-1]:
        at += a.shape[along]
        ends.append(at)
    both = jnp.concatenate(arrays, axis=along)
    return tuple(jnp.split(lax.all_gather(both, axis, axis=dim, tiled=True), ends, axis=along))


def from_everyone(value, axis):
    count = lax.axis_size(axis)
    return lax.all_to_all(
        jnp.broadcast_to(value[None], (count, *value.shape)), axis, 0, 0, tiled=True
    )


def of_everyone(value, axis):
    return from_everyone(value, axis).sum(axis=0)


def joined_along(parts, dim):
    parts = jnp.moveaxis(parts, 0, dim)
    lengths = parts.shape
    return parts.reshape(*lengths[:dim], lengths[dim] * lengths[dim + 1], *lengths[dim + 2 :])


def gather_directly(value, axis, dim):
    return joined_along(from_everyone(value, axis), dim)


def of_everyone_2(value, axis):
    everything = from_everyone(value, axis)
    return jnp.sum(everything.astype(jnp.float32), axis=0)


def cut_along(value, dim, count):
    lengths = value.shape
    parts = value.reshape(*lengths[:dim], count, lengths[dim] // count, *lengths[dim + 1 :])
    return jnp.moveaxis(parts, dim, 0)


def summed_on_arrival(value, axis, dim):
    count = lax.axis_size(axis)
    parts = lax.all_to_all(cut_along(value, dim, count), axis, 0, 0, tiled=True)
    return jnp.sum(parts, axis=0)


def together(arrays, axis):
    ends = [0]
    for a in arrays:
        ends.append(ends[-1] + a.size)
    subtotal = of_everyone(jnp.concatenate([a.ravel() for a in arrays]), axis)
    return tuple((subtotal[b:e].reshape(a.shape) for a, b, e in zip(arrays, ends, ends[1:])))


def apply_rotary(tensor, length):
    half_dim = tensor.shape[-1] // 2
    positions = jnp.arange(length, dtype=jnp.float32)
    inv_freq = jnp.exp(
        jnp.arange(half_dim, dtype=jnp.float32) * (-2.0 * math.log(500000.0) / tensor.shape[-1])
    )
    angles = positions[:, None] * inv_freq[None, :]
    cosine_table = jnp.cos(angles)[:, None, :]
    sine_table = jnp.sin(angles)[:, None, :]
    lower_half = tensor[..., :half_dim]
    upper_half = tensor[..., half_dim:]
    return jnp.concatenate(
        [
            lower_half * cosine_table - upper_half * sine_table,
            upper_half * cosine_table + lower_half * sine_table,
        ],
        axis=-1,
    )


def per_device(
    tokens,
    attn_gain,
    w_query,
    key_projection_weight,
    value_projection_weight,
    w_out,
    final_gain,
    unembed,
    clean_ids,
    corrupt_ids,
):
    row_count = tokens.shape[0]
    seq_count = row_count // SEQUENCE_LENGTH
    gathered = lax.all_gather(tokens, "mp", axis=1, tiled=True)
    wide = gathered.astype(jnp.float32)
    normalized_rows = (
        wide
        * lax.rsqrt(jnp.mean(wide * wide, axis=1, keepdims=True) + 1e-05)
        * attn_gain.astype(jnp.float32)
    ).astype(jnp.bfloat16)
    weight_pieces = side_by_side(
        (w_query, key_projection_weight, value_projection_weight), "dp", 0, 1
    )
    query_raw, key_raw, value_raw = tuple(
        (
            jnp.dot(normalized_rows, weight_piece, preferred_element_type=jnp.float32)
            for weight_piece in weight_pieces
        )
    )
    q_heads = query_raw.shape[1] // HEAD_SIZE
    kv_heads = key_raw.shape[1] // HEAD_SIZE
    query_group_width = q_heads // kv_heads
    queries = apply_rotary(
        query_raw.reshape(seq_count, SEQUENCE_LENGTH, q_heads, HEAD_SIZE), SEQUENCE_LENGTH
    ).astype(jnp.bfloat16)
    projected_key_rows = apply_rotary(
        key_raw.reshape(seq_count, SEQUENCE_LENGTH, kv_heads, HEAD_SIZE), SEQUENCE_LENGTH
    ).astype(jnp.bfloat16)
    value_rows = value_raw.astype(jnp.bfloat16).reshape(
        seq_count, SEQUENCE_LENGTH, kv_heads, HEAD_SIZE
    )
    grouped = queries.reshape(seq_count, SEQUENCE_LENGTH, kv_heads, query_group_width, HEAD_SIZE)
    logits = jnp.einsum(
        "btkgd,bskd->bkgts", grouped, projected_key_rows, preferred_element_type=jnp.float32
    ) / math.sqrt(HEAD_SIZE)
    causal = jnp.arange(SEQUENCE_LENGTH)[:, None] >= jnp.arange(SEQUENCE_LENGTH)[None, :]
    logits = jnp.where(causal, logits, -1e30)
    row_top = jnp.max(logits, axis=-1, keepdims=True)
    exponent = jnp.exp(logits - row_top)
    attn_probs = (exponent / jnp.sum(exponent, axis=-1, keepdims=True)).astype(jnp.bfloat16)
    mixed_heads = jnp.einsum(
        "bkgts,bskd->btkgd", attn_probs, value_rows, preferred_element_type=jnp.float32
    )
    head_out = mixed_heads.astype(jnp.bfloat16).reshape(row_count, q_heads * HEAD_SIZE)
    totals = jnp.sum(head_out.astype(jnp.float32), axis=0)
    all_totals = of_everyone(totals, "dp")
    head_mean = all_totals / (row_count * lax.axis_size("dp"))
    last_out = head_out.reshape(seq_count, SEQUENCE_LENGTH, q_heads * HEAD_SIZE)[
        :, SEQUENCE_LENGTH - 1, :
    ]
    every_last = gather_directly(last_out, "dp", 0)
    partial_out = jnp.dot(every_last, w_out, preferred_element_type=jnp.float32)
    summed_out = of_everyone_2(partial_out.astype(jnp.bfloat16), "mp").astype(jnp.float32)
    moved_out = lax.all_to_all(
        summed_out.astype(jnp.bfloat16), "dp", split_axis=0, concat_axis=1, tiled=True
    )
    span = moved_out.shape[1] // lax.axis_size("mp")
    attn_last = lax.dynamic_slice_in_dim(moved_out, lax.axis_index("mp") * span, span, 1)
    last_tokens = tokens.reshape(seq_count, SEQUENCE_LENGTH, tokens.shape[1])[
        :, SEQUENCE_LENGTH - 1, :
    ].astype(jnp.float32)
    residual = last_tokens + attn_last.astype(jnp.float32)
    vocab_rows = unembed.shape[0]
    id_range = lax.axis_index("dp") * vocab_rows + jnp.arange(vocab_rows, dtype=jnp.int32)
    one_hot = (clean_ids[:, None] == id_range[None, :]).astype(jnp.float32) - (
        corrupt_ids[:, None] == id_range[None, :]
    ).astype(jnp.float32)
    direction = summed_on_arrival(
        jnp.dot(one_hot.astype(jnp.bfloat16), unembed, preferred_element_type=jnp.float32), "dp", 0
    )
    weighted = final_gain.astype(jnp.float32) * direction
    square_part, product_part = together(
        (jnp.sum(residual * residual, axis=1), jnp.sum(residual * weighted, axis=1)), "mp"
    )
    inverse = lax.rsqrt(square_part / MODEL_WIDTH + 1e-05)
    metric = inverse * product_part
    grad_last = (
        weighted * inverse[:, None] - residual * (metric * inverse * inverse / MODEL_WIDTH)[:, None]
    ).astype(jnp.bfloat16)
    grad_full = gather_directly(grad_last, "mp", 1)
    grad_seqs = lax.all_to_all(grad_full, "dp", split_axis=1, concat_axis=0, tiled=True)
    head_grads = summed_on_arrival(
        lax.dot_general(
            grad_seqs, w_out, (((1,), (1,)), ((), ())), preferred_element_type=jnp.float32
        ),
        "dp",
        0,
    )
    mean_gap = head_mean[None, :] - last_out.astype(jnp.float32)
    scores = jnp.sum((mean_gap * head_grads).reshape(seq_count, q_heads, HEAD_SIZE), axis=2)
    return (head_out, scores, metric)


def solution(mesh):
    in_specs = (
        P("dp", "mp"),
        P(),
        P("dp", "mp"),
        P("dp", "mp"),
        P("dp", "mp"),
        P("mp", "dp"),
        P("mp"),
        P("dp", "mp"),
        P(),
        P(),
    )
    out_specs = (P("dp", "mp"), P("dp", "mp"), P("dp"))
    return jax.shard_map(
        per_device, mesh=mesh, in_specs=in_specs, out_specs=out_specs, check_vma=False
    )
```

profile of v0, /device:TPU:2, one launch (start us, length us, event | category | flops | bytes accessed | tf_op | source)
XLA Modules:
  0.0 637.6 jit_solution(4554884628780977542)
XLA Ops:
  8.0 1.7 pad_maximum_fusion
  11.0 68.3 %all-gather.3.cloned.1.call-done = bf16[256,8192]{1,0:T(8,128)(2,1)} async-done(((bf16[256,2048]{1,0:T(8,128)(2,1)}), bf16[256,8192]{1,0:T(8,128)(2,1)}) %all-gather.3.cloned.1.call-update) | async-done | bytes 4194320 | tf_op jit(solution)/shard_map/all_gather | solution.py:101
  79.4 3.1 fusion.2
  82.5 380.6 %all-gather.5.cloned.1.call-done = bf16[8192,1280]{1,0:T(8,128)(2,1)} async-done(((bf16[128,1280]{1,0:T(8,128)(2,1)}), bf16[8192,1280]{1,0:T(8,128)(2,1)}) %all-gather.5.cloned.1.call-update) | async-done | bytes 20971536 | tf_op jit(solution)/shard_map/all_gather | solution.py:18
  463.0 9.4 %fusion.10 = f32[32,8,8,128]{3,1,2,0:T(8,128)S(1)} fusion(bf16[8192,1280]{1,0:T(8,128)(2,1)} %all-gather.5.cloned.1.call-done, bf16[256,8192]{1,0:T(8,128)(2,1)} %all-gather.3.cloned.1.call-done, f32[8192]{0:T(1024)S(1)} %convert_element_type.90, f32[256]{0:T(256)S(1)} %add_rsqrt_fusion), kind=kOutput, calls=%fused_computation.16 | convolution fusion | flops 4303355904 | bytes 22053888 | tf_op jit(solution)/shard_map/dot_general | solution.py:113
  473.0 1.6 copy-done.1
  474.6 3.3 fusion.13
  479.7 4.8 convert_reduce_fusion
  487.6 10.2 %all-to-all-start.2 = ((bf16[64,2,512]{2,1,0:T(2,128)(2,1)}), bf16[64,2,512]{2,1,0:T(2,128)(2,1)S(1)}, u32[]{:S(2)}, u32[]{:S(2)}) async-start(bf16[64,2,512]{2,1,0:T(2,128)(2,1)} %reshape.299), calls=%async_computation.2 | async-start | bytes 262144 | tf_op jit(solution)/shard_map/all_to_all | solution.py:23
  497.8 3.1 convolution_bitcast_fusion
  502.2 5.4 all-to-all-done.2
  507.6 5.5 all-to-all-start.1
  513.4 12.6 %all-to-all-done.1 = f32[64,1,2048]{2,1,0:T(1,128)S(1)} async-done(((f32[64,1,2048]{2,1,0:T(1,128)}), f32[64,1,2048]{2,1,0:T(1,128)S(1)}, u32[]{:S(2)}, u32[]{:S(2)}) %all-to-all-start.1) | async-done | bytes 524320 | tf_op jit(solution)/shard_map/all_to_all | solution.py:55
  526.7 4.9 all-to-all-start.3
  531.9 7.7 %all-to-all-done.3 = bf16[4,64,128]{2,1,0:T(8,128)(2,1)S(1)} async-done(((bf16[4,64,128]{2,1,0:T(8,128)(2,1)}), bf16[4,64,128]{2,1,0:T(8,128)(2,1)S(1)}, u32[]{:S(2)}, u32[]{:S(2)}) %all-to-all-start.3) | async-done | bytes 65568 | tf_op jit(solution)/shard_map/all_to_all | solution.py:23
  540.3 5.9 all-to-all-start.4
  546.3 9.0 %all-to-all-done.4 = bf16[64,1,128]{2,1,0:T(2,128)(2,1)S(1)} async-done(((bf16[64,1,128]{2,1,0:T(2,128)(2,1)}), bf16[64,1,128]{2,1,0:T(2,128)(2,1)S(1)}, u32[]{:S(2)}, u32[]{:S(2)}) %all-to-all-start.4) | async-done | bytes 16416 | tf_op jit(solution)/shard_map/all_to_all | solution.py:151
  558.1 10.0 %all_to_all.69 = f32[4,1,2]{2,1,0:T(1,128)S(1)} all-to-all(f32[4,1,2]{2,1,0:T(1,128)S(1)} %broadcast_in_dim.31), channel_id=1, replica_groups=mesh['dp'=64,'mp'=4] {'mp'}, dimensions={0} | all-to-all | bytes 64 | tf_op jit(solution)/shard_map/all_to_all | solution.py:23
  570.9 10.1 %all_to_all.70 = bf16[4,2,1024]{2,1,0:T(2,128)(2,1)S(1)} all-to-all(bf16[4,2,1024]{2,1,0:T(2,128)(2,1)S(1)} %reshape.301), channel_id=1, replica_groups=mesh['dp'=64,'mp'=4] {'mp'}, dimensions={0} | all-to-all | bytes 32768 | tf_op jit(solution)/shard_map/all_to_all | solution.py:23
  581.0 14.0 %all_to_all.71 = bf16[1,64,128]{2,0,1:T(2,128)(2,1)S(1)} all-to-all(bf16[1,64,128]{2,0,1:T(2,128)(2,1)S(1)} %bitcast.88), channel_id=1, replica_groups=mesh['dp'=64,'mp'=4] {'dp'}, dimensions={1} | all-to-all | bytes 32768 | tf_op jit(solution)/shard_map/all_to_all | solution.py:178
  595.8 5.5 all-to-all-start
  602.5 9.7 %all-to-all-done = f32[64,1,1024]{2,1,0:T(1,128)S(1)} async-done(((f32[64,1,1024]{2,1,0:T(1,128)}), f32[64,1,1024]{2,1,0:T(1,128)S(1)}, u32[]{:S(2)}, u32[]{:S(2)}) %all-to-all-start) | async-done | bytes 262176 | tf_op jit(solution)/shard_map/all_to_all | solution.py:23
  612.3 5.8 all-to-all-start.8
  619.4 9.4 %all-to-all-done.8 = f32[64,1,1024]{2,1,0:T(1,128)S(1)} async-done(((f32[64,1,1024]{2,1,0:T(1,128)}), f32[64,1,1024]{2,1,0:T(1,128)S(1)}, u32[]{:S(2)}, u32[]{:S(2)}) %all-to-all-start.8) | async-done | bytes 262176 | tf_op jit(solution)/shard_map/all_to_all | solution.py:55
  (57 shorter events, 19.0 us)
Async XLA Ops:
  7.2 506.0 %copy-start = (bf16[1024,128]{1,0:T(8,128)(2,1)S(1)}, bf16[1024,128]{1,0:T(8,128)(2,1)}, u32[]{:S(2)}) copy-start(bf16[1024,128]{1,0:T(8,128)(2,1)} %param.15) | copy-start | bytes 786436
  7.2 72.2 %all-gather.3.cloned.1.call-start = ((), (), s32[]{:S(2)}) async-start(), calls=%async_computation.9 | async-start | bytes 5242880 | tf_op jit(solution)/shard_map/all_gather | solution.py:101
  7.9 455.1 %all-gather.5.cloned.1.call-start = ((), (), s32[]{:S(2)}) async-start(), calls=%async_computation.10 | async-start | bytes 21299200 | tf_op jit(solution)/shard_map/all_gather | solution.py:18
  472.4 2.2 copy-start.1
  479.7 18.1 %copy-start.3 = (s32[64]{0:T(128)S(1)}, s32[64]{0:T(128)}, u32[]{:S(2)}) copy-start(s32[64]{0:T(128)} %param.19) | copy-start | bytes 772
  479.7 18.1 %copy-start.4 = (s32[64]{0:T(128)S(1)}, s32[64]{0:T(128)}, u32[]{:S(2)}) copy-start(s32[64]{0:T(128)} %param.18) | copy-start | bytes 772
  487.6 20.0 %all-to-all-start.2 = ((bf16[64,2,512]{2,1,0:T(2,128)(2,1)}), bf16[64,2,512]{2,1,0:T(2,128)(2,1)S(1)}, u32[]{:S(2)}, u32[]{:S(2)}) async-start(bf16[64,2,512]{2,1,0:T(2,128)(2,1)} %reshape.299), calls=%async_computation.2 | async-start | bytes 262144 | tf_op jit(solution)/shard_map/all_to_all | solution.py:23
  497.8 48.5 %copy-start.2 = (bf16[2048]{0:T(1024)(128)(2,1)S(1)}, bf16[2048]{0:T(1024)(128)(2,1)}, u32[]{:S(2)}) copy-start(bf16[2048]{0:T(1024)(128)(2,1)} %param.16) | copy-start | bytes 12292
  507.6 18.5 %all-to-all-start.1 = ((f32[64,1,2048]{2,1,0:T(1,128)}), f32[64,1,2048]{2,1,0:T(1,128)S(1)}, u32[]{:S(2)}, u32[]{:S(2)}) async-start(f32[64,1,2048]{2,1,0:T(1,128)} %copy.63), calls=%async_computation.1 | async-start | bytes 1048576 | tf_op jit(solution)/shard_map/all_to_all | solution.py:55
  526.7 13.0 %all-to-all-start.3 = ((bf16[4,64,128]{2,1,0:T(8,128)(2,1)}), bf16[4,64,128]{2,1,0:T(8,128)(2,1)S(1)}, u32[]{:S(2)}, u32[]{:S(2)}) async-start(bf16[4,64,128]{2,1,0:T(8,128)(2,1)} %broadcast_in_dim.30), calls=%async_computation.3 | async-start | bytes 131072 | tf_op jit(solution)/shard_map/all_to_all | solution.py:23
  540.3 15.0 %all-to-all-start.4 = ((bf16[64,1,128]{2,1,0:T(2,128)(2,1)}), bf16[64,1,128]{2,1,0:T(2,128)(2,1)S(1)}, u32[]{:S(2)}, u32[]{:S(2)}) async-start(bf16[64,1,128]{2,1,0:T(2,128)(2,1)} %copy.64), calls=%async_computation.4 | async-start | bytes 65536 | tf_op jit(solution)/shard_map/all_to_all | solution.py:151
  595.8 16.4 %all-to-all-start = ((f32[64,1,1024]{2,1,0:T(1,128)}), f32[64,1,1024]{2,1,0:T(1,128)S(1)}, u32[]{:S(2)}, u32[]{:S(2)}) async-start(f32[64,1,1024]{2,1,0:T(1,128)} %broadcast_in_dim.27), calls=%async_computation | async-start | bytes 524288 | tf_op jit(solution)/shard_map/all_to_all | solution.py:23
  612.3 16.6 %all-to-all-start.8 = ((f32[64,1,1024]{2,1,0:T(1,128)}), f32[64,1,1024]{2,1,0:T(1,128)S(1)}, u32[]{:S(2)}, u32[]{:S(2)}) async-start(f32[64,1,1024]{2,1,0:T(1,128)} %copy.67), calls=%async_computation.8 | async-start | bytes 524288 | tf_op jit(solution)/shard_map/all_to_all | solution.py:55
Sparse Core Ops, SparseCore 0:
  9.8 69.4 all-gather.2
  81.7 381.2 all-gather.4
where the time goes:
time: 639 us; the launch traced here: 638 us
  waiting for transfers between devices  504 us (79%)
  starting transfers between devices  37.9 us (6%)
  blocking collectives  34.1 us (5%)
  matrix products  21.6 us (3%)
  between operations  16.8 us (3%)
  other arithmetic  13.7 us (2%)
  local copies, waits for them, and re-layouts  9.94 us (2%)
    all_gather x1, waiting for transfers between devices, side_by_side(): lax.all_gather(both, axis, axis=dim, tiled=True)  381 us
    all_gather x1, waiting for transfers between devices, per_device(): gathered = lax.all_gather(tokens, 'mp', axis=1, tiled=True)  68.3 us
    all_to_all x3, waiting for transfers between devices, from_everyone(): lax.all_to_all(jnp.broadcast_to(value[None], (count, *value.shape)), axis...  22.8 us
    all_to_all x2, waiting for transfers between devices, summed_on_arrival(): parts = lax.all_to_all(cut_along(value, dim, count), axis, 0, 0, tiled=True)  22.1 us
    all_to_all x3, starting transfers between devices, from_everyone(): lax.all_to_all(jnp.broadcast_to(value[None], (count, *value.shape)), axis...  20.6 us
    all_to_all x2, blocking collectives, from_everyone(): lax.all_to_all(jnp.broadcast_to(value[None], (count, *value.shape)), axis...  20.1 us
    all_to_all x1, blocking collectives, per_device(): lax.all_to_all(grad_full, 'dp', split_axis=1, concat_axis=0, tiled=True)  14 us
  transfers between devices with their start and end apart: 8, of which 8 were waited for; matrix products, arithmetic and copies ran while one was open for 2% of the time, Pallas kernels for 0%

commit v1 on v0

--- a/solution.py
+++ b/solution.py
@@ -3,6 +3,7 @@
 import jax.numpy as jnp
 from jax import lax
 from jax.sharding import PartitionSpec as P
+from jax.lax import all_to_all, axis_size
 
 MODEL_WIDTH = 8192
 HEAD_SIZE = 128
@@ -98,7 +99,12 @@
 ):
     row_count = tokens.shape[0]
     seq_count = row_count // SEQUENCE_LENGTH
-    gathered = lax.all_gather(tokens, "mp", axis=1, tiled=True)
+    pieces_in = []
+    for _ in range(axis_size("mp")):
+        pieces_in.append(tokens)
+    block_now = jnp.stack(pieces_in)
+    extra = all_to_all(block_now, axis_name="mp", split_axis=0, concat_axis=0)
+    gathered = jnp.concatenate(extra, axis=1)
     wide = gathered.astype(jnp.float32)
     normalized_rows = (
         wide

time: 639 us -> 669 us (1.047)
  local copies, waits for them, and re-layouts: 9.94 us -> 52.5 us
  waiting for transfers between devices: 504 us -> 475 us
  starting transfers between devices: 37.9 us -> 45.8 us
    all_to_all x0 -> x1, waiting for transfers between devices: none -> 96.3 us  [per_device(): extra = all_to_all(block_now, axis_name='mp', split_axis=0, concat_axis=0)]
    all_gather x1 -> x0, waiting for transfers between devices: 68.3 us -> none  [per_device(): gathered = lax.all_gather(tokens, 'mp', axis=1, tiled=True)]
    all_gather x1, waiting for transfers between devices: 381 us -> 325 us  [side_by_side(): lax.all_gather(both, axis, axis=dim, tiled=True)]
    dot_general x0 -> x2, local copies, waits for them, and re-layouts: none -> 34.8 us  [per_device(): jnp.dot(normalized_rows, weight_piece, preferred_element_type=jnp.float32)]
    convert_element_type x0 -> x2, other arithmetic: none -> 8.86 us  [the longest x1 6.31 us: per_device(): wide = gathered.astype(jnp.float32)]
    all_to_all x0 -> x1, starting transfers between devices: none -> 8.59 us  [per_device(): extra = all_to_all(block_now, axis_name='mp', split_axis=0, concat_axis=0)]
  transfers between devices with their start and end apart: 8 -> 8, of which waited for: 8 -> 8; matrix products, arithmetic and copies ran while one was open for 2% -> 4% of each run, Pallas kernels for 0% -> 0%
where the time goes in v1:
time: 669 us; the launch traced here: 667 us
  waiting for transfers between devices  475 us (71%)
  local copies, waits for them, and re-layouts  52.5 us (8%)
  starting transfers between devices  45.8 us (7%)
  blocking collectives  34.1 us (5%)
  matrix products  23.2 us (3%)
  other arithmetic  19.4 us (3%)
  between operations  16.8 us (3%)
    all_gather x1, waiting for transfers between devices, side_by_side(): lax.all_gather(both, axis, axis=dim, tiled=True)  325 us
    all_to_all x1, waiting for transfers between devices, per_device(): extra = all_to_all(block_now, axis_name='mp', split_axis=0, concat_axis=0)  96.3 us
    dot_general x2, local copies, waits for them, and re-layouts, per_device(): jnp.dot(normalized_rows, weight_piece, preferred_element_type=jnp.float32)  34.8 us
    all_to_all x3, waiting for transfers between devices, from_everyone(): lax.all_to_all(jnp.broadcast_to(value[None], (count, *value.shape)), axis...  22.8 us
    all_to_all x2, waiting for transfers between devices, summed_on_arrival(): parts = lax.all_to_all(cut_along(value, dim, count), axis, 0, 0, tiled=True)  22.1 us
    all_to_all x2, blocking collectives, from_everyone(): lax.all_to_all(jnp.broadcast_to(value[None], (count, *value.shape)), axis...  20.1 us
    all_to_all x3, starting transfers between devices, from_everyone(): lax.all_to_all(jnp.broadcast_to(value[None], (count, *value.shape)), axis...  19.9 us
    dot_general x2, matrix products, per_device(): jnp.dot(normalized_rows, weight_piece, preferred_element_type=jnp.float32)  14.6 us
  transfers between devices with their start and end apart: 8, of which 8 were waited for; matrix products, arithmetic and copies ran while one was open for 4% of the time, Pallas kernels for 0%

profile of v1, /device:TPU:2, one launch (start us, length us, event | category | flops | bytes accessed | tf_op | source)
XLA Modules:
  0.0 667.1 jit_solution(8106063644781515319)
XLA Ops:
  12.8 8.6 %all-to-all-start = ((bf16[4,256,2048]{2,1,0:T(8,128)(2,1)}), bf16[4,256,2048]{2,1,0:T(8,128)(2,1)}, u32[]{:S(2)}, u32[]{:S(2)}) async-start(bf16[4,256,2048]{2,1,0:T(8,128)(2,1)} %stack.4), calls=%async_computation | async-start | bytes 8388608 | tf_op jit(solution)/shard_map/all_to_all | solution.py:106
  21.7 96.3 %all-to-all-done = bf16[4,256,2048]{2,1,0:T(8,128)(2,1)} async-done(((bf16[4,256,2048]{2,1,0:T(8,128)(2,1)}), bf16[4,256,2048]{2,1,0:T(8,128)(2,1)}, u32[]{:S(2)}, u32[]{:S(2)}) %all-to-all-start) | async-done | bytes 4194336 | tf_op jit(solution)/shard_map/all_to_all | solution.py:106
  118.0 6.2 copy.60
  124.2 6.3 convert_element_type.168
  134.2 325.1 %all-gather.2.cloned.1.call-done = bf16[8192,1280]{1,0:T(8,128)(2,1)} async-done(((bf16[128,1280]{1,0:T(8,128)(2,1)}), bf16[8192,1280]{1,0:T(8,128)(2,1)}) %all-gather.2.cloned.1.call-update) | async-done | bytes 20971536 | tf_op jit(solution)/shard_map/all_gather | solution.py:19
  459.3 13.9 %slice_bitcast_fusion = bf16[1024,8192]{0,1:T(8,128)(2,1)} fusion(bf16[8192,1280]{1,0:T(8,128)(2,1)} %all-gather.2.cloned.1.call-done), kind=kLoop, calls=%fused_computation | loop fusion | bytes 33554432 | tf_op jit(solution)/shard_map/dot_general | solution.py:119
  473.2 20.9 %copy.61 = bf16[1024,8192]{1,0:T(8,128)(2,1)} copy(bf16[1024,8192]{0,1:T(8,128)(2,1)} %slice_bitcast_fusion) | data formatting | bytes 33554432 | tf_op jit(solution)/shard_map/dot_general | solution.py:119
  498.3 10.7 %fusion.12 = f32[1,256,8,128]{1,3,2,0:T(8,128)S(1)} fusion(bf16[8,128,8192]{2,1,0:T(8,128)(2,1)} %bitcast.105, f32[256,1,1,1,8192]{0,4,3,2,1:T(8,128)} %bitcast.106, f32[8192]{0:T(1024)S(1)} %convert_element_type.141, f32[256]{0:T(256)S(1)} %add_rsqrt_fusion), kind=kOutput, calls=%fused_computation.19 | convolution fusion | flops 4301258752 | bytes 26248192 | tf_op jit(solution)/shard_map/dot_general | solution.py:119
  510.0 4.7 convert_reduce_fusion
  517.7 9.9 %all-to-all-start.3 = ((bf16[64,2,512]{2,1,0:T(2,128)(2,1)}), bf16[64,2,512]{2,1,0:T(2,128)(2,1)S(1)}, u32[]{:S(2)}, u32[]{:S(2)}) async-start(bf16[64,2,512]{2,1,0:T(2,128)(2,1)} %reshape.382), calls=%async_computation.3 | async-start | bytes 262144 | tf_op jit(solution)/shard_map/all_to_all | solution.py:24
  532.1 5.4 all-to-all-done.3
  537.4 5.5 all-to-all-start.2
  543.3 12.6 %all-to-all-done.2 = f32[64,1,2048]{2,1,0:T(1,128)S(1)} async-done(((f32[64,1,2048]{2,1,0:T(1,128)}), f32[64,1,2048]{2,1,0:T(1,128)S(1)}, u32[]{:S(2)}, u32[]{:S(2)}) %all-to-all-start.2) | async-done | bytes 524320 | tf_op jit(solution)/shard_map/all_to_all | solution.py:56
  556.6 4.5 all-to-all-start.4
  561.4 7.7 %all-to-all-done.4 = bf16[4,64,128]{2,1,0:T(8,128)(2,1)S(1)} async-done(((bf16[4,64,128]{2,1,0:T(8,128)(2,1)}), bf16[4,64,128]{2,1,0:T(8,128)(2,1)S(1)}, u32[]{:S(2)}, u32[]{:S(2)}) %all-to-all-start.4) | async-done | bytes 65568 | tf_op jit(solution)/shard_map/all_to_all | solution.py:24
  569.7 5.9 all-to-all-start.5
  575.7 9.0 %all-to-all-done.5 = bf16[64,1,128]{2,1,0:T(2,128)(2,1)S(1)} async-done(((bf16[64,1,128]{2,1,0:T(2,128)(2,1)}), bf16[64,1,128]{2,1,0:T(2,128)(2,1)S(1)}, u32[]{:S(2)}, u32[]{:S(2)}) %all-to-all-start.5) | async-done | bytes 16416 | tf_op jit(solution)/shard_map/all_to_all | solution.py:157
  587.5 10.0 %all_to_all.74 = f32[4,1,2]{2,1,0:T(1,128)S(1)} all-to-all(f32[4,1,2]{2,1,0:T(1,128)S(1)} %broadcast_in_dim.31), channel_id=1, replica_groups=mesh['dp'=64,'mp'=4] {'mp'}, dimensions={0} | all-to-all | bytes 64 | tf_op jit(solution)/shard_map/all_to_all | solution.py:24
  600.3 10.1 %all_to_all.75 = bf16[4,2,1024]{2,1,0:T(2,128)(2,1)S(1)} all-to-all(bf16[4,2,1024]{2,1,0:T(2,128)(2,1)S(1)} %reshape.384), channel_id=1, replica_groups=mesh['dp'=64,'mp'=4] {'mp'}, dimensions={0} | all-to-all | bytes 32768 | tf_op jit(solution)/shard_map/all_to_all | solution.py:24
  610.4 14.0 %all_to_all.76 = bf16[1,64,128]{2,0,1:T(2,128)(2,1)S(1)} all-to-all(bf16[1,64,128]{2,0,1:T(2,128)(2,1)S(1)} %bitcast.110), channel_id=1, replica_groups=mesh['dp'=64,'mp'=4] {'dp'}, dimensions={1} | all-to-all | bytes 32768 | tf_op jit(solution)/shard_map/all_to_all | solution.py:184
  625.3 5.5 all-to-all-start.1
  632.0 9.7 %all-to-all-done.1 = f32[64,1,1024]{2,1,0:T(1,128)S(1)} async-done(((f32[64,1,1024]{2,1,0:T(1,128)}), f32[64,1,1024]{2,1,0:T(1,128)S(1)}, u32[]{:S(2)}, u32[]{:S(2)}) %all-to-all-start.1) | async-done | bytes 262176 | tf_op jit(solution)/shard_map/all_to_all | solution.py:24
  641.7 5.8 all-to-all-start.9
  648.9 9.4 %all-to-all-done.9 = f32[64,1,1024]{2,1,0:T(1,128)S(1)} async-done(((f32[64,1,1024]{2,1,0:T(1,128)}), f32[64,1,1024]{2,1,0:T(1,128)S(1)}, u32[]{:S(2)}, u32[]{:S(2)}) %all-to-all-start.9) | async-done | bytes 262176 | tf_op jit(solution)/shard_map/all_to_all | solution.py:56
  (62 shorter events, 32.4 us)
Async XLA Ops:
  7.2 535.9 %copy-start = (bf16[1024,128]{1,0:T(8,128)(2,1)S(1)}, bf16[1024,128]{1,0:T(8,128)(2,1)}, u32[]{:S(2)}) copy-start(bf16[1024,128]{1,0:T(8,128)(2,1)} %param.15) | copy-start | bytes 786436
  7.2 452.1 %all-gather.2.cloned.1.call-start = ((), (), s32[]{:S(2)}) async-start(), calls=%async_computation.10 | async-start | bytes 21299200 | tf_op jit(solution)/shard_map/all_gather | solution.py:19
  12.8 8.6 %copy-start.2 = (bf16[8192]{0:T(1024)(128)(2,1)S(1)}, bf16[8192]{0:T(1024)(128)(2,1)}, u32[]{:S(2)}) copy-start(bf16[8192]{0:T(1024)(128)(2,1)} %param.11) | copy-start | bytes 49156
  12.8 105.3 %all-to-all-start = ((bf16[4,256,2048]{2,1,0:T(8,128)(2,1)}), bf16[4,256,2048]{2,1,0:T(8,128)(2,1)}, u32[]{:S(2)}, u32[]{:S(2)}) async-start(bf16[4,256,2048]{2,1,0:T(8,128)(2,1)} %stack.4), calls=%async_computation | async-start | bytes 8388608 | tf_op jit(solution)/shard_map/all_to_all | solution.py:106
  124.2 6.3 copy-start.1
  510.0 17.7 %copy-start.4 = (s32[64]{0:T(128)S(1)}, s32[64]{0:T(128)}, u32[]{:S(2)}) copy-start(s32[64]{0:T(128)} %param.19) | copy-start | bytes 772
  510.0 17.7 %copy-start.5 = (s32[64]{0:T(128)S(1)}, s32[64]{0:T(128)}, u32[]{:S(2)}) copy-start(s32[64]{0:T(128)} %param.18) | copy-start | bytes 772
  517.7 19.7 %all-to-all-start.3 = ((bf16[64,2,512]{2,1,0:T(2,128)(2,1)}), bf16[64,2,512]{2,1,0:T(2,128)(2,1)S(1)}, u32[]{:S(2)}, u32[]{:S(2)}) async-start(bf16[64,2,512]{2,1,0:T(2,128)(2,1)} %reshape.382), calls=%async_computation.3 | async-start | bytes 262144 | tf_op jit(solution)/shard_map/all_to_all | solution.py:24
  527.6 48.0 %copy-start.3 = (bf16[2048]{0:T(1024)(128)(2,1)S(1)}, bf16[2048]{0:T(1024)(128)(2,1)}, u32[]{:S(2)}) copy-start(bf16[2048]{0:T(1024)(128)(2,1)} %param.16) | copy-start | bytes 12292
  537.4 18.5 %all-to-all-start.2 = ((f32[64,1,2048]{2,1,0:T(1,128)}), f32[64,1,2048]{2,1,0:T(1,128)S(1)}, u32[]{:S(2)}, u32[]{:S(2)}) async-start(f32[64,1,2048]{2,1,0:T(1,128)} %copy.69), calls=%async_computation.2 | async-start | bytes 1048576 | tf_op jit(solution)/shard_map/all_to_all | solution.py:56
  556.6 12.5 %all-to-all-start.4 = ((bf16[4,64,128]{2,1,0:T(8,128)(2,1)}), bf16[4,64,128]{2,1,0:T(8,128)(2,1)S(1)}, u32[]{:S(2)}, u32[]{:S(2)}) async-start(bf16[4,64,128]{2,1,0:T(8,128)(2,1)} %broadcast_in_dim.30), calls=%async_computation.4 | async-start | bytes 131072 | tf_op jit(solution)/shard_map/all_to_all | solution.py:24
  569.7 15.0 %all-to-all-start.5 = ((bf16[64,1,128]{2,1,0:T(2,128)(2,1)}), bf16[64,1,128]{2,1,0:T(2,128)(2,1)S(1)}, u32[]{:S(2)}, u32[]{:S(2)}) async-start(bf16[64,1,128]{2,1,0:T(2,128)(2,1)} %copy.70), calls=%async_computation.5 | async-start | bytes 65536 | tf_op jit(solution)/shard_map/all_to_all | solution.py:157
  625.3 16.4 %all-to-all-start.1 = ((f32[64,1,1024]{2,1,0:T(1,128)}), f32[64,1,1024]{2,1,0:T(1,128)S(1)}, u32[]{:S(2)}, u32[]{:S(2)}) async-start(f32[64,1,1024]{2,1,0:T(1,128)} %broadcast_in_dim.27), calls=%async_computation.1 | async-start | bytes 524288 | tf_op jit(solution)/shard_map/all_to_all | solution.py:24
  641.7 16.6 %all-to-all-start.9 = ((f32[64,1,1024]{2,1,0:T(1,128)}), f32[64,1,1024]{2,1,0:T(1,128)S(1)}, u32[]{:S(2)}, u32[]{:S(2)}) async-start(f32[64,1,1024]{2,1,0:T(1,128)} %copy.73), calls=%async_computation.9 | async-start | bytes 524288 | tf_op jit(solution)/shard_map/all_to_all | solution.py:56
Sparse Core Ops, SparseCore 0:
  10.4 448.8 all-gather.1
